TPU v7x, 32 devices: a whole 2x2x4 slice. The times are simulated.
32 devices in a mesh: section: 2 (over core), dp: 16 (over z, y, x).
Axes of the slice: x: 2, y: 2, z: 4, core: 2. Of those that a mesh axis runs over, the one named last changes fastest.
Arguments:
- hidden: bfloat16 [16384, 768], P('dp'), may hold values from -6 to 6
- segment_ids: int32 [32, 512], P('dp'), may hold values from 0 to 3, never falling along the last dimension, each value on 1 to 256 neighbouring positions
- cotangent: bfloat16 [2, 16384, 768], P('section', 'dp'), may hold values from -6 to 6
- w_qkv: bfloat16 [2, 768, 2304], P('section'), may hold values from -0.21875 to 0.21875
- w_out: bfloat16 [2, 768, 768], P('section'), may hold values from -2.5 to 2.5
- w_up: bfloat16 [2, 768, 3072], P('section'), may hold values from -0.21875 to 0.21875
- w_down: bfloat16 [2, 3072, 768], P('section'), may hold values from -0.109375 to 0.109375
- biases: float32 [2, 6, 768], P('section'), may hold values from -3 to 3
- gains: float32 [2, 2, 768], P('section'), may hold values from 0.25 to 1.75
- up_bias: float32 [2, 3072], P('section'), may hold values from -3 to 3
Outputs:
- states: bfloat16 [2, 16384, 768], P('section', 'dp')
- grad_input: float32 [16384, 768], P('dp')
- grad_w_qkv: float32 [2, 768, 2304], P('section', 'dp')
- grad_w_out: float32 [2, 768, 768], P('section', 'dp')
- grad_w_up: float32 [2, 768, 3072], P('section', 'dp')
- grad_w_down: float32 [2, 3072, 768], P('section', 'dp')
- grad_biases: float32 [2, 6, 768], P('section', None, 'dp')
- grad_gains: float32 [2, 2, 768], P('section', None, 'dp')
- grad_up_bias: float32 [2, 3072], P('section', 'dp')
Inputs may be any that keep to these rules, and one draw needn't show every extreme that they name: `segment_ids`: in every sequence the ids run through 0 to 3 without falling, each document 1 to 256 tokens, one exactly 256.
All inputs are finite; a program needn't handle non-finite values.
Results may differ from a plain program's by a relative error of at most 0.015.
Values may be sent and summed in bfloat16 or wider, within the bound.
A program may use at most 256 MiB of HBM per device.

v0:
```python
from functools import reduce

import jax
import jax.numpy as jnp
from jax import lax
from jax.sharding import PartitionSpec as P

HEADS = 12
DOCS = 4
MICRO = 2


norm_eps = 1e-12
masked_score = -1e30
inv_root_two = 0.7071067811865476
inv_root_tau = 0.3989422804014327


def shifted(block, axis, distance):
    devices = range(lax.axis_size(axis))
    route = [(i - distance, i) for i in devices if i - distance in devices]
    return lax.ppermute(block, axis, route)


def gelu_value(preact):
    return 0.5 * preact * (1.0 + lax.erf(preact * inv_root_two))


def gelu_slope(preact):
    return (
        0.5 * (1.0 + lax.erf(preact * inv_root_two))
        + preact * jnp.exp(-0.5 * preact * preact) * inv_root_tau
    )


def layer_norm(residue):
    centered = residue - jnp.mean(residue, axis=-1, keepdims=True)
    inv_std = lax.rsqrt(jnp.mean(centered * centered, axis=-1, keepdims=True) + norm_eps)
    return (centered * inv_std, inv_std)


def norm_back(gradient, normed, inv_std):
    return inv_std * (
        gradient
        - jnp.mean(gradient, axis=-1, keepdims=True)
        - normed * jnp.mean(gradient * normed, axis=-1, keepdims=True)
    )


def times_transposed(left_side, right_side):
    return lax.dot_general(
        left_side, right_side, (((1,), (1,)), ((), ())), preferred_element_type=jnp.float32
    )


def outer_sum(left_side, right_side):
    return lax.dot_general(
        left_side, right_side, (((0,), (0,)), ((), ())), preferred_element_type=jnp.float32
    )


def split_into_heads(matrix):
    return matrix.reshape(matrix.shape[0], HEADS, -1)


def score_table(query_per_head, key_per_head, segments):
    score_scale = query_per_head.shape[-1] ** (-0.5)
    unscaled_scores = (
        jnp.einsum("syn,byn->ysb", query_per_head, key_per_head, preferred_element_type=jnp.float32)
        * score_scale
    )
    same_doc = segments[:, None] == segments[None, :]
    return jnp.where(same_doc[None], unscaled_scores, masked_score)


def attend_forward(operands):
    queries, key_rows, value_rows, segments = operands
    scores = score_table(split_into_heads(queries), split_into_heads(key_rows), segments)
    maximum = jnp.max(scores, axis=-1, keepdims=True)
    log_total = maximum + jnp.log(jnp.sum(jnp.exp(scores - maximum), axis=-1, keepdims=True))
    reduced_weight = jnp.exp(scores - log_total).astype(jnp.bfloat16)
    attention_result = jnp.einsum(
        "zea,azq->ezq",
        reduced_weight,
        split_into_heads(value_rows),
        preferred_element_type=jnp.float32,
    )
    return (attention_result.reshape(queries.shape).astype(jnp.bfloat16), log_total[..., 0])


def attend_backward(operands):
    queries, key_rows, value_rows, segments, log_total, grad_low = operands
    query_per_head = split_into_heads(queries)
    key_per_head = split_into_heads(key_rows)
    value_per_head = split_into_heads(value_rows)
    head_gradient = split_into_heads(grad_low)
    score_scale = query_per_head.shape[-1] ** (-0.5)
    scores = score_table(query_per_head, key_per_head, segments)
    attention_weight = jnp.exp(scores - log_total[..., None])
    grad_weights = jnp.einsum(
        "syn,byn->ysb", head_gradient, value_per_head, preferred_element_type=jnp.float32
    )
    score_gradient = (
        attention_weight
        * (grad_weights - jnp.sum(attention_weight * grad_weights, axis=-1, keepdims=True))
    ).astype(jnp.bfloat16)
    grad_query = (
        jnp.einsum("zea,azq->ezq", score_gradient, key_per_head, preferred_element_type=jnp.float32)
        * score_scale
    )
    grad_key = (
        jnp.einsum(
            "tfa,ftc->atc", score_gradient, query_per_head, preferred_element_type=jnp.float32
        )
        * score_scale
    )
    grad_value = jnp.einsum(
        "tfa,ftc->atc",
        attention_weight.astype(jnp.bfloat16),
        head_gradient,
        preferred_element_type=jnp.float32,
    )
    row_shape = queries.shape
    return (
        grad_query.reshape(row_shape),
        grad_key.reshape(row_shape),
        grad_value.reshape(row_shape),
    )


def block_forward(inputs, segments, params):
    w_qkv, w_out, w_up, w_down, biases, gains, up_bias = params
    model_width = inputs.shape[1]
    seq_count, length = segments.shape
    projected = jnp.dot(inputs, w_qkv, preferred_element_type=jnp.float32)
    queries = (projected[:, :model_width] + biases[0]).astype(jnp.bfloat16)
    key_rows = projected[:, model_width : 2 * model_width].astype(jnp.bfloat16)
    value_rows = (projected[:, 2 * model_width :] + biases[1]).astype(jnp.bfloat16)
    by_seq = (
        queries.reshape(seq_count, length, model_width),
        key_rows.reshape(seq_count, length, model_width),
        value_rows.reshape(seq_count, length, model_width),
        segments,
    )
    attention_result, log_total = lax.map(attend_forward, by_seq)
    attention_result = attention_result.reshape(-1, model_width)
    mixed_out = jnp.dot(attention_result, w_out, preferred_element_type=jnp.float32) + biases[2]
    normed_one, inv_one = layer_norm(inputs.astype(jnp.float32) + mixed_out)
    hidden = normed_one * gains[0] + biases[3]
    hidden_low = hidden.astype(jnp.bfloat16)
    preact = jnp.dot(hidden_low, w_up, preferred_element_type=jnp.float32) + up_bias
    active_low = gelu_value(preact).astype(jnp.bfloat16)
    ffn_out = jnp.dot(active_low, w_down, preferred_element_type=jnp.float32) + biases[4]
    normed_two, inv_two = layer_norm(hidden + ffn_out)
    result = normed_two * gains[1] + biases[5]
    stored = (
        inputs,
        queries,
        key_rows,
        value_rows,
        log_total,
        attention_result,
        normed_one,
        inv_one,
        hidden_low,
        preact,
        active_low,
        normed_two,
        inv_two,
    )
    return (result, stored)


def block_backward(gradient, stored, segments, params):
    w_qkv, w_out, w_up, w_down, biases, gains, up_bias = params
    (
        inputs,
        queries,
        key_rows,
        value_rows,
        log_total,
        attention_result,
        normed_one,
        inv_one,
        hidden_low,
        preact,
        active_low,
        normed_two,
        inv_two,
    ) = stored
    model_width = inputs.shape[1]
    seq_count, length = segments.shape
    gain_two = jnp.sum(gradient * normed_two, axis=0)
    shift_two = jnp.sum(gradient, axis=0)
    resid_two = norm_back(gradient * gains[1], normed_two, inv_two)
    ffn_low = resid_two.astype(jnp.bfloat16)
    grad_pre = times_transposed(ffn_low, w_down) * gelu_slope(preact)
    pre_low = grad_pre.astype(jnp.bfloat16)
    grad_hidden = resid_two + times_transposed(pre_low, w_up)
    gain_one = jnp.sum(grad_hidden * normed_one, axis=0)
    shift_one = jnp.sum(grad_hidden, axis=0)
    resid_one = norm_back(grad_hidden * gains[0], normed_one, inv_one)
    mixed_low = resid_one.astype(jnp.bfloat16)
    attend_low = times_transposed(mixed_low, w_out).astype(jnp.bfloat16)

    def as_seqs(matrix):
        return matrix.reshape(seq_count, length, model_width)

    grad_query, grad_key, grad_value = lax.map(
        attend_backward,
        (
            as_seqs(queries),
            as_seqs(key_rows),
            as_seqs(value_rows),
            segments,
            log_total,
            as_seqs(attend_low),
        ),
    )
    grad_query = grad_query.reshape(-1, model_width)
    grad_key = grad_key.reshape(-1, model_width)
    grad_value = grad_value.reshape(-1, model_width)
    proj_low = jnp.concatenate([grad_query, grad_key, grad_value], axis=1).astype(jnp.bfloat16)
    grad_inputs = resid_one + times_transposed(proj_low, w_qkv)
    bias_grads = jnp.stack(
        [
            jnp.sum(grad_query, axis=0),
            jnp.sum(grad_value, axis=0),
            jnp.sum(resid_one, axis=0),
            shift_one,
            jnp.sum(resid_two, axis=0),
            shift_two,
        ]
    )
    gain_grads = jnp.stack([gain_one, gain_two])
    small_grads = (bias_grads, gain_grads, jnp.sum(grad_pre, axis=0))
    pieces = (
        inputs,
        proj_low,
        attention_result,
        mixed_low,
        hidden_low,
        pre_low,
        active_low,
        ffn_low,
    )
    return (grad_inputs, small_grads, pieces)


def weight_products(pieces):
    inputs, proj_low, attention_result, mixed_low, hidden_low, pre_low, active_low, ffn_low = pieces
    return (
        outer_sum(inputs, proj_low),
        outer_sum(attention_result, mixed_low),
        outer_sum(hidden_low, pre_low),
        outer_sum(active_low, ffn_low),
    )


def doc_starts(segments):
    doc_ids = jnp.arange(DOCS, dtype=jnp.int32)
    return jnp.sum((segments[:, None, :] < doc_ids[None, :, None]).astype(jnp.int32), axis=-1)


def first_marks(segments):
    leading = jnp.ones((segments.shape[0], 1), dtype=jnp.bool_)
    return jnp.concatenate([leading, segments[:, 1:] != segments[:, :-1]], axis=1)


def pick_rows(matrix, starts):
    return jnp.take_along_axis(matrix, starts[..., None], axis=1)


def spread_rows(cls_table, segments):
    return jnp.take_along_axis(cls_table, segments[..., None], axis=1)


def fetch(stacked, position):
    return jax.tree.map(
        lambda member: lax.dynamic_index_in_dim(member, position, 0, False), stacked
    )


def add_trees(left_side, right_side):
    return jax.tree.map(jnp.add, left_side, right_side)


def local(hidden, segment_ids, cotangent, w_qkv, w_out, w_up, w_down, biases, gains, up_bias):
    params = (w_qkv[0], w_out[0], w_up[0], w_down[0], biases[0], gains[0], up_bias[0])
    section_id = lax.axis_index("section")
    on_head = section_id == 1
    seq_count = segment_ids.shape[0] // MICRO
    length = segment_ids.shape[1]
    row_count = seq_count * length
    model_width = hidden.shape[1]

    def segments_of(mb_index):
        return lax.dynamic_slice_in_dim(segment_ids, mb_index * seq_count, seq_count, 0)

    def rows_of(matrix, mb_index):
        return lax.dynamic_slice_in_dim(matrix, mb_index * row_count, row_count, 0)

    carried = jnp.zeros((seq_count, DOCS, model_width), jnp.bfloat16)
    results = []
    stored_list = []
    for tick_id in range(MICRO + 1):
        mb_index = jnp.clip(tick_id - section_id, 0, MICRO - 1)
        segments = segments_of(mb_index)
        is_first = first_marks(segments).reshape(row_count, 1)
        placed = spread_rows(carried, segments).reshape(row_count, model_width)
        inputs = jnp.where(is_first & on_head, placed, rows_of(hidden, mb_index))
        result, stored = block_forward(inputs, segments, params)
        result_low = result.astype(jnp.bfloat16)
        outgoing = pick_rows(
            result_low.reshape(seq_count, length, model_width), doc_starts(segments)
        )
        carried = shifted(outgoing, "section", 1)
        results.append(result_low)
        stored_list.append(stored)
    result_stack = jnp.stack(results)
    stored_stack = jax.tree.map(lambda *arrays: jnp.stack(arrays), *stored_list)
    coming = jnp.zeros((seq_count, DOCS, model_width), jnp.bfloat16)
    grad_buffer = jnp.zeros((MICRO * row_count, model_width), jnp.float32)
    collected = []
    for tick_id in range(MICRO + 1):
        raw_index = tick_id - 1 + section_id
        is_valid = (raw_index >= 0) & (raw_index < MICRO)
        mb_index = jnp.clip(raw_index, 0, MICRO - 1)
        stored = fetch(stored_stack, mb_index + section_id)
        segments = segments_of(mb_index)
        is_first = first_marks(segments).reshape(row_count, 1)
        returned = spread_rows(coming, segments).reshape(row_count, model_width).astype(jnp.float32)
        gradient = rows_of(cotangent[0], mb_index).astype(jnp.float32) + jnp.where(
            is_first & jnp.logical_not(on_head), returned, 0.0
        )
        grad_inputs, small_grads, pieces = block_backward(gradient, stored, segments, params)
        sending = pick_rows(
            grad_inputs.reshape(seq_count, length, model_width), doc_starts(segments)
        ).astype(jnp.bfloat16)
        coming = shifted(sending, "section", -1)
        kept_rows = jnp.where(is_first & on_head, 0.0, grad_inputs)
        kept_rows = jnp.where(is_valid, kept_rows, 0.0)
        previous = rows_of(grad_buffer, mb_index)
        grad_buffer = lax.dynamic_update_slice_in_dim(
            grad_buffer, previous + kept_rows, mb_index * row_count, 0
        )
        tick_grads = weight_products(pieces) + small_grads
        collected.append(jax.tree.map(lambda member: jnp.where(is_valid, member, 0.0), tick_grads))
    totals = reduce(add_trees, collected)
    grad_qkv, grad_out, grad_up, grad_down, grad_biases, grad_gains, grad_up_bias = totals
    totals = (
        lax.psum_scatter(grad_qkv, "dp", scatter_dimension=0, tiled=True),
        lax.psum_scatter(grad_out, "dp", scatter_dimension=0, tiled=True),
        lax.psum_scatter(grad_up, "dp", scatter_dimension=0, tiled=True),
        lax.psum_scatter(grad_down, "dp", scatter_dimension=0, tiled=True),
        lax.psum_scatter(grad_biases, "dp", scatter_dimension=1, tiled=True),
        lax.psum_scatter(grad_gains, "dp", scatter_dimension=1, tiled=True),
        lax.psum_scatter(grad_up_bias, "dp", scatter_dimension=0, tiled=True),
    )
    grad_input = lax.psum(grad_buffer.astype(jnp.bfloat16), "section").astype(jnp.float32)
    states = jnp.concatenate(
        [
            lax.dynamic_index_in_dim(result_stack, mb_number + section_id, 0, False)
            for mb_number in range(MICRO)
        ],
        axis=0,
    )
    return (states[None], grad_input) + tuple((member[None] for member in totals))


def solution(mesh):
    placed = (
        P("dp", None),
        P("dp", None),
        P("section", "dp", None),
        P("section", None, None),
        P("section", None, None),
        P("section", None, None),
        P("section", None, None),
        P("section", None, None),
        P("section", None, None),
        P("section", None),
    )
    return jax.shard_map(
        local,
        mesh=mesh,
        in_specs=placed,
        out_specs=(
            P("section", "dp", None),
            P("dp", None),
            P("section", "dp", None),
            P("section", "dp", None),
            P("section", "dp", None),
            P("section", "dp", None),
            P("section", None, "dp"),
            P("section", None, "dp"),
            P("section", "dp"),
        ),
        check_vma=False,
    )
```

profile of v0, /device:TPU:0, one launch (start us, length us, event | category | flops | bytes accessed | tf_op | source)
XLA Modules:
  0.0 1397.4 jit_solution(7831705670133476271)
XLA Ops:
  34.7 3.5 fusion
  38.2 3.5 exponential_reduce_fusion.2
  41.9 4.5 fusion.176
  47.8 19.1 %add_bitcast_fusion.2 = (f32[1,512,3072]{2,1,0:T(8,128)}, bf16[512,3072]{1,0:T(8,128)(2,1)S(1)}) fusion(f32[3072]{0:T(1024)S(1)} %bitcast.874, bf16[1,768,3072]{2,1,0:T(8,128)(2,1)} %param.21, f32[512,768]{1,0:T(8,128)S(1)} %get-tuple-element.323, f32[768]{0:T(1024)S(1)} %copy-done.119, f32[768]{0:T(1024)S(1)} %get-tuple-element.214, ...), kind=kOutput, calls=%fused_computation.86 | convolution fusion | flops 2427322368 | bytes 15751168 | tf_op jit(solution)/shard_map/dot_general | solution.py:151
  125.1 3.5 fusion.1
  128.6 3.5 exponential_reduce_fusion.1
  132.2 4.5 fusion.175
  138.2 7.5 add_bitcast_fusion.1
  174.0 3.5 fusion.2
  177.5 3.5 exponential_reduce_fusion
  181.1 4.7 fusion.174
  187.2 5.9 add_bitcast_fusion
  195.7 3.7 slice_bitcast_fusion.2
  211.8 6.8 pad_maximum_fusion
  218.6 8.6 fusion.303
  228.8 7.0 fusion.132
  264.4 4.1 bitcast_convert_fusion.4
  268.5 6.8 multiply_reduce_fusion.2
  275.3 7.4 multiply_convert_fusion.2
  289.6 3.3 select_dynamic-update-slice_fusion
  308.8 7.9 fusion.317
  316.7 6.4 fusion.318
  343.2 3.5 fusion.128
  349.5 8.6 fusion.302
  358.2 3.5 fusion.124
  367.9 9.2 bitcast_convert_fusion.2
  377.2 11.5 multiply_reduce_fusion.1
  390.0 7.0 multiply_convert_fusion.1
  401.5 4.8 add_dynamic-update-slice_fusion.1
  428.9 3.5 fusion.120
  435.6 8.6 fusion.301
  444.2 3.5 fusion.116
  454.0 9.4 bitcast_convert_fusion
  463.5 11.2 multiply_reduce_fusion
  476.1 7.0 multiply_convert_fusion
  503.2 5.9 add_dynamic-update-slice_fusion
  527.1 7.6 select_add_fusion.2
  543.2 10.0 select_add_fusion.1
  553.5 6.1 pad_maximum_fusion.1
  559.8 9.7 fusion.81
  569.7 6.8 fusion.79
  576.5 10.1 select_add_fusion
  591.7 77.6 %all-reduce = f32[3072]{0:T(1024)} all-reduce(f32[3072]{0:T(1024)S(1)} %select_add_fusion.5), channel_id=8, replica_groups=mesh['section'=2,'dp'=16] {'dp'}, use_global_device_ids=true, to_apply=%region_71.75.clone | all-reduce | flops 3072 | bytes 24576
  672.1 76.5 %reduce-scatter.19.cloned.1.call-done = f32[48,6]{1,0:T(8,128)} async-done(((f32[768,6]{1,0:T(8,128)}), f32[48,6]{1,0:T(8,128)}) %reduce-scatter.19.cloned.1.call-update) | async-done | bytes 1168
  753.2 128.1 %reduce-scatter.13.cloned.1.call-done = f32[48,768]{1,0:T(8,128)} async-done(((f32[768,768]{1,0:T(8,128)}), f32[48,768]{1,0:T(8,128)}) %reduce-scatter.13.cloned.1.call-update) | async-done | bytes 147472 | tf_op jit(solution)/shard_map/reduce_scatter | solution.py:353
  881.4 155.3 %reduce-scatter.11.cloned.1.call-done = f32[48,2304]{1,0:T(8,128)} async-done(((f32[768,2304]{1,0:T(8,128)}), f32[48,2304]{1,0:T(8,128)}) %reduce-scatter.11.cloned.1.call-update) | async-done | bytes 442384 | tf_op jit(solution)/shard_map/reduce_scatter | solution.py:352
  1036.7 175.7 %reduce-scatter.15.cloned.1.call-done = f32[48,3072]{1,0:T(8,128)} async-done(((f32[768,3072]{1,0:T(8,128)}), f32[48,3072]{1,0:T(8,128)}) %reduce-scatter.15.cloned.1.call-update) | async-done | bytes 589840 | tf_op jit(solution)/shard_map/reduce_scatter | solution.py:354
  1212.4 177.4 %reduce-scatter.17.cloned.1.call-done = f32[192,768]{1,0:T(8,128)} async-done(((f32[3072,768]{1,0:T(8,128)}), f32[192,768]{1,0:T(8,128)}) %reduce-scatter.17.cloned.1.call-update) | async-done | bytes 589840 | tf_op jit(solution)/shard_map/reduce_scatter | solution.py:355
  (658 shorter events, 310.9 us)
Async XLA Ops:
  8.0 14.6 %copy-start = (bf16[1,768,2304]{2,1,0:T(8,128)(2,1)S(1)}, bf16[1,768,2304]{2,1,0:T(8,128)(2,1)}, u32[]{:S(2)}) copy-start(bf16[1,768,2304]{2,1,0:T(8,128)(2,1)} %param.19) | copy-start | bytes 10616836
  8.0 662.7 %reduce-scatter.21.cloned.1.call-start = ((), (), s32[]{:S(2)}) async-start(), calls=%async_computation.12 | async-start | bytes 417792
  14.3 11.4 copy-start.93
  14.3 56.4 %copy-start.90 = (f32[768]{0:T(1024)}, f32[768]{0:T(1024)S(1)}, u32[]{:S(2)}) copy-start(f32[768]{0:T(1024)S(1)} %get-tuple-element.207) | copy-start | bytes 9220
  41.8 25.1 %copy-start.88 = (f32[768]{0:T(1024)}, f32[768]{0:T(1024)S(1)}, u32[]{:S(2)}) copy-start(f32[768]{0:T(1024)S(1)} %get-tuple-element.214) | copy-start | bytes 9220
  41.8 28.9 %copy-start.80 = (f32[768]{0:T(1024)}, f32[768]{0:T(1024)S(1)}, u32[]{:S(2)}) copy-start(f32[768]{0:T(1024)S(1)} %get-tuple-element.213) | copy-start | bytes 9220
  47.4 19.5 %copy-start.35 = (f32[512,768]{1,0:T(8,128)}, f32[512,768]{1,0:T(8,128)S(1)}, u32[]{:S(2)}) copy-start(f32[512,768]{1,0:T(8,128)S(1)} %get-tuple-element.323) | copy-start | bytes 4718596
  47.4 19.5 %copy-start.110 = (f32[512]{0:T(512)}, f32[512]{0:T(512)S(1)}, u32[]{:S(2)}) copy-start(f32[512]{0:T(512)S(1)} %broadcast_multiply_fusion.17) | copy-start | bytes 6148
  47.4 19.5 %slice-start.16 = ((s8[4718592]{0:T(1024)(128)(4,1)}), s8[4194304]{0:T(1024)(128)(4,1)S(1)}, s32[]{:S(2)}) async-start(s8[4718592]{0:T(1024)(128)(4,1)} %bitcast.860), calls=%async_computation.29 | async-start | bytes 8388608
  47.8 19.2 %copy-start.114 = (f32[512]{0:T(512)}, f32[512]{0:T(512)S(1)}, u32[]{:S(2)}) copy-start(f32[512]{0:T(512)S(1)} %add_rsqrt_fusion.5) | copy-start | bytes 6148
  47.8 19.2 %copy-start.152 = (f32[768]{0:T(1024)S(1)}, f32[768]{0:T(1024)}, u32[]{:S(2)}) copy-start(f32[768]{0:T(1024)} %get-tuple-element.212) | copy-start | bytes 9220
  47.8 19.2 %slice-start.17 = ((s8[4718592]{0:T(1024)(128)(4,1)}), s8[524288]{0:T(1024)(128)(4,1)S(1)}, s32[]{:S(2)}) async-start(s8[4718592]{0:T(1024)(128)(4,1)} %bitcast.860), calls=%async_computation.30 | async-start | bytes 1048576
  75.7 32.4 %collective-permute-start = (bf16[1,4,768]{2,1,0:T(4,128)(2,1)}, bf16[1,4,768]{2,1,0:T(4,128)(2,1)S(1)}, u32[]{:S(2)}, u32[]{:S(2)}) collective-permute-start(bf16[1,4,768]{2,1,0:T(4,128)(2,1)} %bitcast_select_fusion.12), channel_id=1, source_target_pairs={{0,16},{1,17},{2,18},{3,19},{4,20},{5,21},{6,22},{7,23},{8,24},{9,... | collective-permute-start | bytes 18440 | tf_op jit(solution)/shard_map/ppermute | solution.py:22
  153.3 3.7 collective-permute-start.1
  185.8 13.5 slice-start.20
  187.2 12.1 slice-start.21
  193.2 18.5 %slice-start.14 = ((s8[6291456]{0:T(1024)(128)(4,1)}), s8[4194304]{0:T(1024)(128)(4,1)S(1)}, s32[]{:S(2)}) async-start(s8[6291456]{0:T(1024)(128)(4,1)} %bitcast.770), calls=%async_computation.27 | async-start | bytes 8388608
  199.4 12.4 slice-start.15
  204.9 13.6 copy-start.1
  268.5 20.5 %copy-start.171 = (bf16[512,12,64]{0,2,1:T(8,128)(2,1)}, bf16[512,12,64]{0,2,1:T(8,128)(2,1)S(1)}, u32[]{:S(2)}) copy-start(bf16[512,12,64]{0,2,1:T(8,128)(2,1)S(1)} %get-tuple-element.339) | copy-start | bytes 2359300
  296.1 44.0 %collective-permute-start.2 = (bf16[1,4,768]{2,1,0:T(4,128)(2,1)}, bf16[1,4,768]{2,1,0:T(4,128)(2,1)S(1)}, u32[]{:S(2)}, u32[]{:S(2)}) collective-permute-start(bf16[1,4,768]{2,1,0:T(4,128)(2,1)} %fusion.234), channel_id=1, source_target_pairs={{16,0},{17,1},{18,2},{19,3},{20,4},{21,5},{22,6},{23,7},{24,8},{25... | collective-permute-start | bytes 18440 | tf_op jit(solution)/shard_map/ppermute | solution.py:22
  343.2 14.9 %slice-start.22 = ((s8[4718592]{0:T(1024)(128)(4,1)}), s8[4194304]{0:T(1024)(128)(4,1)S(1)}, s32[]{:S(2)}) async-start(s8[4718592]{0:T(1024)(128)(4,1)} %bitcast.866), calls=%async_computation.35 | async-start | bytes 8388608
  346.8 11.4 slice-start.8
  377.1 24.4 %copy-start.173 = (bf16[512,12,64]{0,2,1:T(8,128)(2,1)}, bf16[512,12,64]{0,2,1:T(8,128)(2,1)S(1)}, u32[]{:S(2)}) copy-start(bf16[512,12,64]{0,2,1:T(8,128)(2,1)S(1)} %get-tuple-element.348) | copy-start | bytes 2359300
  377.1 11.6 slice-start.3
  377.2 11.5 slice-start.4
  377.2 12.8 slice-start.5
  409.7 15.9 %collective-permute-start.3 = (bf16[1,4,768]{2,1,0:T(4,128)(2,1)}, bf16[1,4,768]{2,1,0:T(4,128)(2,1)S(1)}, u32[]{:S(2)}, u32[]{:S(2)}) collective-permute-start(bf16[1,4,768]{2,1,0:T(4,128)(2,1)} %fusion.233), channel_id=1, source_target_pairs={{16,0},{17,1},{18,2},{19,3},{20,4},{21,5},{22,6},{23,7},{24,8},{25... | collective-permute-start | bytes 18440 | tf_op jit(solution)/shard_map/ppermute | solution.py:22
  428.9 15.3 %slice-start.10 = ((s8[4718592]{0:T(1024)(128)(4,1)}), s8[4194304]{0:T(1024)(128)(4,1)S(1)}, s32[]{:S(2)}) async-start(s8[4718592]{0:T(1024)(128)(4,1)} %bitcast.746), calls=%async_computation.23 | async-start | bytes 8388608
  428.9 15.2 %slice-start.24 = ((s8[4718592]{0:T(1024)(128)(4,1)}), s8[4194304]{0:T(1024)(128)(4,1)S(1)}, s32[]{:S(2)}) async-start(s8[4718592]{0:T(1024)(128)(4,1)} %bitcast.868), calls=%async_computation.37 | async-start | bytes 8388608
  463.4 11.3 slice-start
  463.4 11.2 slice-start.1
  463.5 12.6 slice-start.2
  498.6 249.9 %reduce-scatter.19.cloned.1.call-start = ((), (), s32[]{:S(2)}) async-start(), calls=%async_computation.11 | async-start | bytes 417792
  503.1 246.8 %all-reduce.3.cloned.1.call-start = ((), (), s32[]{:S(2)}) async-start(), calls=%async_computation.6 | async-start | bytes 3145728 | tf_op jit(solution)/shard_map/psum | solution.py:360
  512.3 369.1 %reduce-scatter.13.cloned.1.call-start = ((), (), s32[]{:S(2)}) async-start(), calls=%async_computation.8 | async-start | bytes 2506752 | tf_op jit(solution)/shard_map/reduce_scatter | solution.py:353
  519.7 517.0 %reduce-scatter.11.cloned.1.call-start = ((), (), s32[]{:S(2)}) async-start(), calls=%async_computation.7 | async-start | bytes 7520256 | tf_op jit(solution)/shard_map/reduce_scatter | solution.py:352
  534.7 677.7 %reduce-scatter.15.cloned.1.call-start = ((), (), s32[]{:S(2)}) async-start(), calls=%async_computation.9 | async-start | bytes 10027008 | tf_op jit(solution)/shard_map/reduce_scatter | solution.py:354
  553.2 836.5 %reduce-scatter.17.cloned.1.call-start = ((), (), s32[]{:S(2)}) async-start(), calls=%async_computation.10 | async-start | bytes 10027008 | tf_op jit(solution)/shard_map/reduce_scatter | solution.py:355
  553.5 16.0 %slice-start.6 = ((s8[4718592]{0:T(1024)(128)(4,1)}), s8[4194304]{0:T(1024)(128)(4,1)S(1)}, s32[]{:S(2)}) async-start(s8[4718592]{0:T(1024)(128)(4,1)} %bitcast.742), calls=%async_computation.19 | async-start | bytes 8388608
  559.8 9.8 copy-start.7
  559.8 9.7 slice-start.7
  559.8 9.7 copy-start.18
  559.8 9.7 copy-start.130
  559.8 9.7 copy-start.140
  559.8 9.7 copy-start.142
  559.8 9.7 copy-start.145
  559.8 9.7 copy-start.151
  (165 other events, 717.2 us)
Sparse Core Ops, SparseCore 0:
  498.7 124.4 reduce-scatter.20
  627.9 120.6 reduce-scatter.18
  754.8 126.5 reduce-scatter.12
  887.1 149.5 reduce-scatter.10
  1042.8 169.5 reduce-scatter.14
  1219.4 170.2 reduce-scatter.16
Sparse Core Ops, SparseCore 1:
  512.4 22.9 all-reduce.2
where the time goes:
time: 1400 us
  waiting for transfers between devices  713 us (51%)
  matrix products  274 us (20%)
  other arithmetic  155 us (11%)
  local copies, waits for them, and re-layouts  152 us (11%)
  blocking collectives  77.6 us (6%)
  between operations  19 us (1%)
    reduce_scatter x1, waiting for transfers between devices, local(): lax.psum_scatter(grad_down, 'dp', scatter_dimension=0, tiled=True)  177 us
    reduce_scatter x1, waiting for transfers between devices, local(): lax.psum_scatter(grad_up, 'dp', scatter_dimension=0, tiled=True)  176 us
    reduce_scatter x1, waiting for transfers between devices, local(): lax.psum_scatter(grad_qkv, 'dp', scatter_dimension=0, tiled=True)  155 us
    reduce_scatter x1, waiting for transfers between devices, local(): lax.psum_scatter(grad_out, 'dp', scatter_dimension=0, tiled=True)  128 us
    unnamed x1, blocking collectives  77.6 us
    unnamed x9, waiting for transfers between devices  76.6 us
    dot_general x12, matrix products, times_transposed(): lax.dot_general(left_side, right_side, (((1,), (1,)), ((), ())), preferre...  59.1 us
    dot_general x12, matrix products, outer_sum(): lax.dot_general(left_side, right_side, (((0,), (0,)), ((), ())), preferre...  57.6 us
  transfers between devices with their start and end apart: 11, of which 5 were waited for; matrix products, arithmetic and copies ran while one was open for 13% of the time, Pallas kernels for 0%

commit v1 on v0

v1 whole, which is shorter than its diff:
```python
import functools

import jax
import jax.numpy as jnp
from jax import lax
from jax.experimental import pallas as pl
from jax.experimental.pallas import tpu as pltpu
from jax.sharding import PartitionSpec as P

HEADS = 12
HEAD = 64
NORM_EPS = 1e-12
MASKED = -1e30
INV_ROOT_TWO = 0.7071067811865476
INV_ROOT_TAU = 0.3989422804014327
MESH = pl.DeviceIdType.MESH
BF = jnp.bfloat16
F32 = jnp.float32
TILE = 256
ROWS = 128
VMEM_BYTES = 60 * 1024 * 1024


def dot_nn(a, b):
    return lax.dot_general(a, b, (((1,), (0,)), ((), ())), preferred_element_type=F32)


def dot_nt(a, b):
    return lax.dot_general(a, b, (((1,), (1,)), ((), ())), preferred_element_type=F32)


def dot_tn(a, b):
    return lax.dot_general(a, b, (((0,), (0,)), ((), ())), preferred_element_type=F32)


def loop(count, body):
    def step(i, carry):
        body(i)
        return carry

    lax.fori_loop(0, count, step, 0)


def tile_of(i, size=TILE):
    return pl.ds(pl.multiple_of(i * size, size), size)


class Weights:
    def __init__(self, block, pairs, targets, sems):
        self.waits = []
        own = lax.axis_index("section") == block
        for n, ((mine, theirs), target) in enumerate(zip(pairs, targets)):
            sem = sems.at[n]

            @pl.when(own)
            def _():
                pltpu.make_async_copy(mine, target, sem).start()

            @pl.when(jnp.logical_not(own))
            def _():
                pltpu.make_async_copy(theirs, target, sem).start()

            self.waits.append(pltpu.make_async_copy(mine, target, sem))

    def wait(self, n):
        self.waits[n].wait()


def normed_rows(residue):
    centered = residue - jnp.mean(residue, axis=-1, keepdims=True)
    inv = lax.rsqrt(jnp.mean(centered * centered, axis=-1, keepdims=True) + NORM_EPS)
    return centered * inv, inv


def lane_masks(shape):
    lane = lax.broadcasted_iota(jnp.int32, shape, 1)
    return (lane < HEAD, lane >= HEAD)


def forward_kernel(
    block,
    x_ref, segr_ref, segc_ref, first_ref, qkvb_ref, small_ref, upb_ref,
    wqkv_m, wqkv_t, wout_m, wout_t, wup_m, wup_t, wdown_m, wdown_t,
    qkv_ref, o_ref, lse_ref, n1_ref, inv1_ref, hlow_ref, g_ref, slope_ref, n2_ref, inv2_ref, y_ref, x1_ref,
    wqkv, wout, wup, wdown, mask_ref, res_ref, h_ref, sems,
):
    rows, width = x_ref.shape
    hidden_width = wup.shape[1]
    weights = Weights(
        block,
        ((wqkv_m, wqkv_t), (wout_m, wout_t), (wup_m, wup_t), (wdown_m, wdown_t)),
        (wqkv, wout, wup, wdown),
        sems,
    )
    mask_ref[...] = jnp.where(segc_ref[...] == segr_ref[...], 0.0, MASKED)
    weights.wait(0)
    x = x_ref[...]

    def project(j):
        cols = tile_of(j)
        scale = jnp.where(j < width // TILE, HEAD ** -0.5, 1.0)
        qkv_ref[:, cols] = ((dot_nn(x_ref[...], wqkv[:, cols]) + qkvb_ref[:, cols]) * scale).astype(BF)

    loop(3 * width // TILE, project)

    def attend(pair):
        queries = qkv_ref[:, tile_of(pair, 128)]
        keys = qkv_ref[:, pl.ds(pl.multiple_of(width + pair * 128, 128), 128)]
        values = qkv_ref[:, pl.ds(pl.multiple_of(2 * width + pair * 128, 128), 128)]
        masks = lane_masks((rows, 128))
        parts = []
        for h in range(2):
            scores = dot_nt(keys, jnp.where(masks[h], queries, jnp.zeros_like(queries))) + mask_ref[...]
            top = jnp.max(scores, axis=0, keepdims=True)
            weight = jnp.exp(scores - top)
            total = jnp.sum(weight, axis=0, keepdims=True)
            lse_ref[pair, pl.ds(h, 1), :] = top + jnp.log(total)
            result = dot_tn(values, weight.astype(BF))
            parts.append(result[h * HEAD : (h + 1) * HEAD] * (1.0 / total))
        o_ref[:, tile_of(pair, 128)] = jnp.concatenate(parts, axis=0).T.astype(BF)

    loop(HEADS // 2, attend)
    weights.wait(1)

    def mix(j):
        cols = tile_of(j)
        res_ref[:, cols] = x_ref[:, cols].astype(F32) + (dot_nn(o_ref[...], wout[:, cols]) + small_ref[2:3, cols])

    loop(width // TILE, mix)

    def norm_one(i):
        r = tile_of(i, ROWS)
        normed, inv = normed_rows(res_ref[r, :])
        n1_ref[r, :] = normed
        inv1_ref[r, :] = jnp.broadcast_to(inv, (ROWS, 128))
        h = normed * small_ref[6:7, :] + small_ref[3:4, :]
        h_ref[r, :] = h
        hlow_ref[r, :] = h.astype(BF)

    loop(rows // ROWS, norm_one)
    weights.wait(2)

    def widen(j):
        cols = tile_of(j)
        z = dot_nn(hlow_ref[...], wup[:, cols]) + upb_ref[:, cols]
        half = 0.5 * (1.0 + lax.erf(z * INV_ROOT_TWO))
        g_ref[:, cols] = (z * half).astype(BF)
        slope_ref[:, cols] = (half + z * jnp.exp(-0.5 * z * z) * INV_ROOT_TAU).astype(BF)

    loop(hidden_width // TILE, widen)
    weights.wait(3)

    def narrow(j):
        cols = tile_of(j)
        res_ref[:, cols] = h_ref[:, cols] + (dot_nn(g_ref[...], wdown[:, cols]) + small_ref[4:5, cols])

    loop(width // TILE, narrow)

    def norm_two(i):
        r = tile_of(i, ROWS)
        normed, inv = normed_rows(res_ref[r, :])
        n2_ref[r, :] = normed
        inv2_ref[r, :] = jnp.broadcast_to(inv, (ROWS, 128))
        y = (normed * small_ref[7:8, :] + small_ref[5:6, :]).astype(BF)
        y_ref[r, :] = y
        x1_ref[r, :] = jnp.where(first_ref[r, :] > 0.5, y.astype(F32), x_ref[r, :].astype(F32)).astype(BF)

    loop(rows // ROWS, norm_two)


def norm_back(gradient, normed, inv):
    return inv * (
        gradient
        - jnp.mean(gradient, axis=-1, keepdims=True)
        - normed * jnp.mean(gradient * normed, axis=-1, keepdims=True)
    )


def column_sum(v):
    return jnp.sum(v, axis=0, keepdims=True)


def backward_kernel(
    block,
    cot_ref, dnext_ref, segr_ref, segc_ref, first_ref, small_ref,
    qkv_ref, o_ref, lse_ref, n1_ref, inv1_ref, slope_ref, n2_ref, inv2_ref,
    wqkv_m, wqkv_t, wout_m, wout_t, wup_m, wup_t, wdown_m, wdown_t,
    dx_ref, dproj_ref, da_ref, dz_ref, df_ref, dsmall_ref, dup_ref,
    wqkv, wout, wup, wdown, mask_ref, dr_ref, dh_ref, do_ref, sems,
):
    rows, width = cot_ref.shape
    hidden_width = wup.shape[1]
    weights = Weights(
        block,
        ((wdown_m, wdown_t), (wup_m, wup_t), (wout_m, wout_t), (wqkv_m, wqkv_t)),
        (wdown, wup, wout, wqkv),
        sems,
    )
    mask_ref[...] = jnp.where(segc_ref[...] == segr_ref[...], 0.0, MASKED)
    dsmall_ref[...] = jnp.zeros_like(dsmall_ref)

    def norm_two(i):
        r = tile_of(i, ROWS)
        gradient = cot_ref[r, :].astype(F32)
        if block == 0:
            back = dnext_ref[r, :].astype(BF).astype(F32)
            gradient = gradient + jnp.where(first_ref[r, :] > 0.5, back, 0.0)
        normed = n2_ref[r, :]
        dr = norm_back(gradient * small_ref[7:8, :], normed, inv2_ref[r, 0:1])
        dr_ref[r, :] = dr
        df_ref[r, :] = dr.astype(BF)
        dsmall_ref[7:8, :] += column_sum(gradient * normed)
        dsmall_ref[5:6, :] += column_sum(gradient)
        dsmall_ref[4:5, :] += column_sum(dr)

    loop(rows // ROWS, norm_two)
    weights.wait(0)

    def narrow(j):
        cols = tile_of(j)
        dz = dot_nt(df_ref[...], wdown[cols, :]) * slope_ref[:, cols].astype(F32)
        dup_ref[:, cols] = column_sum(dz)
        dz_ref[:, cols] = dz.astype(BF)

    loop(hidden_width // TILE, narrow)
    weights.wait(1)

    def widen(j):
        cols = tile_of(j)
        dh_ref[:, cols] = dr_ref[:, cols] + dot_nt(dz_ref[...], wup[cols, :])

    loop(width // TILE, widen)

    def norm_one(i):
        r = tile_of(i, ROWS)
        gradient = dh_ref[r, :]
        normed = n1_ref[r, :]
        dr = norm_back(gradient * small_ref[6:7, :], normed, inv1_ref[r, 0:1])
        dr_ref[r, :] = dr
        da_ref[r, :] = dr.astype(BF)
        dsmall_ref[6:7, :] += column_sum(gradient * normed)
        dsmall_ref[3:4, :] += column_sum(gradient)
        dsmall_ref[2:3, :] += column_sum(dr)

    loop(rows // ROWS, norm_one)
    weights.wait(2)

    def mix(j):
        cols = tile_of(j)
        do_ref[:, cols] = dot_nt(da_ref[...], wout[cols, :]).astype(BF)

    loop(width // TILE, mix)

    def attend(pair):
        here = tile_of(pair, 128)
        key_cols = pl.ds(pl.multiple_of(width + pair * 128, 128), 128)
        value_cols = pl.ds(pl.multiple_of(2 * width + pair * 128, 128), 128)
        queries, keys, values = qkv_ref[:, here], qkv_ref[:, key_cols], qkv_ref[:, value_cols]
        grad = do_ref[:, here]
        masks = lane_masks((rows, 128))
        dq, dk, dv = [], 0.0, 0.0
        for h in range(2):
            head_queries = jnp.where(masks[h], queries, jnp.zeros_like(queries))
            head_grad = jnp.where(masks[h], grad, jnp.zeros_like(grad))
            scores = dot_nt(keys, head_queries) + mask_ref[...]
            weight = jnp.exp(scores - lse_ref[pair, pl.ds(h, 1), :])
            dweight = dot_nt(values, head_grad)
            delta = jnp.sum(weight * dweight, axis=0, keepdims=True)
            dscore = (weight * (dweight - delta)).astype(BF)
            dq.append(dot_tn(keys, dscore)[h * HEAD : (h + 1) * HEAD])
            dk = dk + dot_nn(dscore, head_queries)
            dv = dv + dot_nn(weight.astype(BF), head_grad)
        dq = jnp.concatenate(dq, axis=0).T * (HEAD ** -0.5)
        dsmall_ref[0:1, here] = column_sum(dq)
        dsmall_ref[1:2, here] = column_sum(dv)
        dproj_ref[:, here] = dq.astype(BF)
        dproj_ref[:, key_cols] = dk.astype(BF)
        dproj_ref[:, value_cols] = dv.astype(BF)

    loop(HEADS // 2, attend)
    weights.wait(3)

    def project(j):
        cols = tile_of(j)
        dx = dr_ref[:, cols] + dot_nt(dproj_ref[...], wqkv[cols, :])
        if block == 0:
            dx = dx + jnp.where(first_ref[...] > 0.5, 0.0, dnext_ref[:, cols])
        dx_ref[:, cols] = dx

    loop(width // TILE, project)


def in_vmem(count):
    return [pl.BlockSpec(memory_space=pltpu.VMEM)] * count


def in_hbm(count):
    return [pl.BlockSpec(memory_space=pl.ANY)] * count


def shaped(shape, dtype=F32):
    return jax.ShapeDtypeStruct(shape, dtype)


def block_forward(block, x, segr, segc, first, qkvb, small, upb, weights):
    rows, width = x.shape
    hidden_width = upb.shape[1]
    scratch = [pltpu.VMEM(w.shape, BF) for w in weights[::2]]
    return pl.pallas_call(
        functools.partial(forward_kernel, block),
        out_shape=(
            shaped((rows, 3 * width), BF), shaped((rows, width), BF), shaped((HEADS // 2, 2, rows)),
            shaped((rows, width)), shaped((rows, 128)), shaped((rows, width), BF),
            shaped((rows, hidden_width), BF), shaped((rows, hidden_width), BF),
            shaped((rows, width)), shaped((rows, 128)), shaped((rows, width), BF), shaped((rows, width), BF),
        ),
        in_specs=in_vmem(7) + in_hbm(8),
        out_specs=tuple(in_vmem(12)),
        scratch_shapes=scratch + [
            pltpu.VMEM((rows, rows), F32), pltpu.VMEM((rows, width), F32), pltpu.VMEM((rows, width), F32),
            pltpu.SemaphoreType.DMA((4,)),
        ],
        compiler_params=pltpu.CompilerParams(vmem_limit_bytes=VMEM_BYTES),
        name="forward" + str(block),
    )(x, segr, segc, first, qkvb, small, upb, *weights)


def block_backward(block, cot, dnext, segr, segc, first, small, kept, weights):
    rows, width = cot.shape
    hidden_width = weights[4].shape[1]
    scratch = [pltpu.VMEM(w.shape, BF) for w in weights[::2]]
    return pl.pallas_call(
        functools.partial(backward_kernel, block),
        out_shape=(
            shaped((rows, width)), shaped((rows, 3 * width), BF), shaped((rows, width), BF),
            shaped((rows, hidden_width), BF), shaped((rows, width), BF), shaped((16, width)), shaped((1, hidden_width)),
        ),
        in_specs=in_vmem(14) + in_hbm(8),
        out_specs=tuple(in_vmem(7)),
        scratch_shapes=scratch + [
            pltpu.VMEM((rows, rows), F32), pltpu.VMEM((rows, width), F32), pltpu.VMEM((rows, width), F32),
            pltpu.VMEM((rows, width), BF), pltpu.SemaphoreType.DMA((4,)),
        ],
        compiler_params=pltpu.CompilerParams(vmem_limit_bytes=VMEM_BYTES),
        name="backward" + str(block),
    )(cot, dnext, segr, segc, first, small, *kept, *weights)


ORDERS = {"A": (0, 1, 2, 3), "B": (1, 0, 2, 3), "C": (2, 3, 0, 1), "D": (2, 3, 1, 0)}
KINDS = "ABABABABABCD"
BITS = 4
PARTS = 1 << BITS


def sum_kernel(*refs):
    operands = (refs[0:8], refs[8:16])
    small_ref = refs[16]
    out_qkv, out_out, out_up, out_down, out_small = refs[17:22]
    held = refs[22:30]
    (total, outgoing, r1, r2, r3, r4, small_sum, small_in,
     send, recv, load, small_send, small_recv) = refs[30:]
    received = (r1, r2, r3, r4)
    chunks, share, width = total.shape[0], total.shape[-2], total.shape[-1]
    sec, me = lax.axis_index("section"), lax.axis_index("dp")
    bits = [(me >> k) & 1 for k in range(BITS)]

    def fetch(block, names):
        for n in names:
            for b in range(2):

                @pl.when(block == b)
                def _():
                    pltpu.make_async_copy(operands[b][n], held[n], load.at[n]).start()

    def fetched(names):
        for n in names:
            pltpu.make_async_copy(operands[0][n], held[n], load.at[n]).wait()

    barrier = pltpu.get_barrier_semaphore()
    for k in range(BITS):
        pl.semaphore_signal(barrier, inc=1, device_id={"dp": me ^ (1 << k)}, device_id_type=MESH)
    pl.semaphore_signal(barrier, inc=1, device_id={"section": 1 - sec}, device_id_type=MESH)
    qkv, out, up, down = (0, 1), (2, 3), (4, 5), (6, 7)
    for names in (down, up, qkv, out):
        fetch(1 - sec, names)
    pl.semaphore_wait(barrier, BITS + 1)

    def place(part):
        return tuple((part >> (BITS - 1 - k)) & 1 for k in range(BITS))

    def across(chunk):
        return pltpu.make_async_remote_copy(
            src_ref=outgoing.at[chunk], dst_ref=total.at[chunk],
            send_sem=send.at[chunk, 0], recv_sem=recv.at[chunk, 0],
            device_id={"section": 1 - sec}, device_id_type=MESH,
        )

    def product(target, add, left, left_col, right, right_col, chunk_of):
        for n in range(width // TILE):
            cols = pl.ds(n * TILE, TILE)
            rhs_cols = pl.ds(pl.multiple_of(right_col + n * TILE, TILE), TILE)
            result = dot_tn(held[left][:, pl.ds(pl.multiple_of(left_col, TILE), width)], held[right][:, rhs_cols])
            for piece in range(PARTS):
                chunk, part = chunk_of(piece)
                at = (chunk,) + tuple(part) + (slice(None), cols)
                value = result[piece * share : (piece + 1) * share]
                if add:
                    value = value + target[at].astype(F32)
                target[at] = value.astype(BF)

    def products_wide(add, names, first, count):
        target = total if add else outgoing

        def one(j):
            chunk = first + j
            if add:
                across(chunk).wait()
            product(target, add, names[0], 0, names[1], j * width, lambda piece: (chunk, place(piece)))
            if not add:
                across(chunk).start()

        loop(count, one)

    def products_tall(add, names, first, count):
        target = total if add else outgoing

        def one(j):
            def chunk_of(piece):
                return first + piece % count, place(j * (PARTS // count) + piece // count)

            product(target, add, names[0], j * width, names[1], 0, chunk_of)

        if add:
            for chunk in range(first, first + count):
                across(chunk).wait()
        loop(count, one)
        if not add:
            for chunk in range(first, first + count):
                across(chunk).start()

    def exchange(chunk, phase):
        order = ORDERS[KINDS[chunk]]
        at = [slice(None)] * BITS
        for done in range(phase):
            at[BITS - 1 - order[done]] = bits[order[done]]
        at[BITS - 1 - order[phase]] = 1 - bits[order[phase]]
        return pltpu.make_async_remote_copy(
            src_ref=total.at[(chunk,) + tuple(at)], dst_ref=received[phase].at[chunk],
            send_sem=send.at[chunk, phase + 1], recv_sem=recv.at[chunk, phase + 1],
            device_id={"dp": me ^ (1 << order[phase])}, device_id_type=MESH,
        )

    def take(chunk, phase):
        order = ORDERS[KINDS[chunk]]
        exchange(chunk, phase).wait()

        def one(i):
            at, inner, left = [None] * BITS, [], i
            for done in range(phase + 1):
                at[BITS - 1 - order[done]] = bits[order[done]]
            for d in reversed([d for d in range(BITS) if at[d] is None]):
                at[d] = left % 2
                inner.insert(0, at[d])
                left = left // 2
            at = (chunk,) + tuple(at)
            value = total[at].astype(F32) + received[phase][(chunk,) + tuple(inner)].astype(F32)
            total[at] = value.astype(BF)

        if phase < BITS - 1:
            loop(PARTS >> (phase + 1), one)
            exchange(chunk, phase + 1).start()
        else:
            value = total[(chunk,) + tuple(bits[BITS - 1 - d] for d in range(BITS))].astype(F32)
            value = value + received[phase][chunk].astype(F32)
            if chunk < 3:
                out_qkv[:, chunk * width : (chunk + 1) * width] = value
            elif chunk < 4:
                out_out[...] = value
            elif chunk < 8:
                out_up[:, (chunk - 4) * width : (chunk - 3) * width] = value
            else:
                out_down[(chunk - 8) * share : (chunk - 7) * share, :] = value

    def small_exchange(phase):
        target = {"section": 1 - sec} if phase == 0 else {"dp": me ^ (1 << (phase - 1))}
        source = small_ref.at[1 - sec] if phase == 0 else small_sum.at[phase]
        return pltpu.make_async_remote_copy(
            src_ref=source, dst_ref=small_in.at[phase], send_sem=small_send.at[phase], recv_sem=small_recv.at[phase],
            device_id=target, device_id_type=MESH,
        )

    def small_take(phase):
        small_exchange(phase).wait()
        before = small_ref[sec] if phase == 0 else small_sum[phase]
        if phase < BITS:
            small_sum[phase + 1] = before + small_in[phase]
            small_exchange(phase + 1).start()
        else:
            out_small[...] = before + small_in[phase]

    small_exchange(0).start()
    fetched(down)
    products_tall(False, down, 8, 4)
    fetch(sec, down)
    fetched(up)
    products_wide(False, up, 4, 4)
    fetch(sec, up)
    fetched(down)
    products_tall(True, down, 8, 4)
    for chunk in range(8, 12):
        exchange(chunk, 0).start()
    fetched(qkv)
    products_wide(False, qkv, 0, 3)
    fetch(sec, qkv)
    fetched(up)
    products_wide(True, up, 4, 4)
    for chunk in range(4, 8):
        exchange(chunk, 0).start()
    fetched(out)
    products_wide(False, out, 3, 1)
    fetch(sec, out)
    fetched(qkv)
    products_wide(True, qkv, 0, 3)
    for chunk in range(0, 3):
        exchange(chunk, 0).start()
    fetched(out)
    products_wide(True, out, 3, 1)
    exchange(3, 0).start()
    for phase in range(BITS):
        small_take(phase)
        for chunk in (8, 9, 10, 11, 4, 5, 6, 7, 0, 1, 2, 3):
            take(chunk, phase)
    small_take(BITS)


def sum_products(pieces, small):
    rows, width = pieces[0][0].shape
    hidden_width = pieces[0][6].shape[1]
    share = width // PARTS
    chunks = 2 * hidden_width // width + 4
    return pl.pallas_call(
        sum_kernel,
        out_shape=(
            shaped((share, 3 * width)), shaped((share, width)), shaped((share, hidden_width)),
            shaped((hidden_width // PARTS, width)), shaped((16, width)),
        ),
        in_specs=in_hbm(16) + in_vmem(1),
        out_specs=tuple(in_vmem(5)),
        scratch_shapes=[pltpu.VMEM(piece.shape, BF) for piece in pieces[0]] + [
            pltpu.VMEM((chunks, 2, 2, 2, 2, share, width), BF),
            pltpu.VMEM((chunks, 2, 2, 2, 2, share, width), BF),
            pltpu.VMEM((chunks, 2, 2, 2, share, width), BF),
            pltpu.VMEM((chunks, 2, 2, share, width), BF),
            pltpu.VMEM((chunks, 2, share, width), BF),
            pltpu.VMEM((chunks, share, width), BF),
            pltpu.VMEM((BITS + 1, 16, width), F32),
            pltpu.VMEM((BITS + 1, 16, width), F32),
            pltpu.SemaphoreType.DMA((chunks, BITS + 1)),
            pltpu.SemaphoreType.DMA((chunks, BITS + 1)),
            pltpu.SemaphoreType.DMA((8,)),
            pltpu.SemaphoreType.DMA((BITS + 1,)),
            pltpu.SemaphoreType.DMA((BITS + 1,)),
        ],
        compiler_params=pltpu.CompilerParams(
            collective_id=0, has_side_effects=True, vmem_limit_bytes=VMEM_BYTES
        ),
        name="sum_products",
    )(*pieces[0], *pieces[1], small)


def sum_plainly(pieces, small):
    def scattered(names):
        both = jnp.stack([dot_tn(pieces[b][names[0]], pieces[b][names[1]]) for b in range(2)])
        own = lax.psum_scatter(both, "section", scatter_dimension=0, tiled=False)
        return lax.psum_scatter(own, "dp", scatter_dimension=0, tiled=True)

    own_small = lax.psum(lax.psum_scatter(small, "section", scatter_dimension=0, tiled=False), "dp")
    return tuple(scattered(names) for names in ((0, 1), (2, 3), (4, 5), (6, 7))) + (own_small,)


def swap(value):
    return lax.ppermute(value, "section", [(0, 1), (1, 0)])


def local(hidden, segment_ids, cotangent, w_qkv, w_out, w_up, w_down, biases, gains, up_bias):
    sec, me = lax.axis_index("section"), lax.axis_index("dp")
    count = lax.axis_size("dp")
    length, width = segment_ids.shape[1], hidden.shape[1]
    rows = hidden.shape[0] // 2
    assert rows == length

    def rows_of(matrix, half):
        return lax.dynamic_slice_in_dim(matrix, half * rows, rows, 0)

    def by_block(mine, theirs):
        return jnp.where(sec == 0, mine, theirs), jnp.where(sec == 0, theirs, mine)

    mine = (w_qkv[0], w_out[0], w_up[0], w_down[0])
    weights = []
    for own in mine:
        weights += [own, swap(own)]
    packed = jnp.concatenate([biases[0], gains[0], up_bias[0].reshape(-1, width)], axis=0)
    smalls = by_block(packed, swap(packed))
    cots = by_block(rows_of(cotangent[0], sec), swap(rows_of(cotangent[0], 1 - sec)))
    x = rows_of(hidden, sec)
    segments = lax.dynamic_index_in_dim(segment_ids, sec, 0, False)
    segr, segc = segments.reshape(1, rows), segments.reshape(rows, 1)
    first = jnp.concatenate([jnp.ones((1,), F32), (segments[1:] != segments[:-1]).astype(F32)]).reshape(rows, 1)

    inputs, kept, states = [x], [], []
    for block in range(2):
        small = smalls[block]
        qkvb = jnp.concatenate([small[0:1], jnp.zeros((1, width), F32), small[1:2]], axis=1)
        result = block_forward(block, inputs[block], segr, segc, first, qkvb, small, small[8:].reshape(1, -1), weights)
        kept.append(result[:10])
        states.append(result[10])
        inputs.append(result[11])

    pieces, dsmalls, dnext = [None, None], [None, None], x
    for block in (1, 0):
        qkv, o, lse, n1, inv1, hlow, g, slope, n2, inv2 = kept[block]
        dnext, dproj, da, dz, df, dsmall, dup = block_backward(
            block, cots[block], dnext, segr, segc, first, smalls[block],
            (qkv, o, lse, n1, inv1, slope, n2, inv2), weights,
        )
        pieces[block] = (inputs[block], dproj, o, da, hlow, dz, g, df)
        dsmalls[block] = jnp.concatenate([dsmall[:8], dup.reshape(-1, width), jnp.zeros((4, width), F32)], axis=0)
    small = jnp.stack(dsmalls)
    fits = count == PARTS and width % (16 * PARTS) == 0
    sums = (sum_products if fits else sum_plainly)(pieces, small)
    gqkv, gout, gup, gdown, gsmall = sums
    share, up_share = width // count, up_bias.shape[1] // count
    columns = lax.dynamic_slice_in_dim(gsmall[:8], me * share, share, 1)
    gup_bias = lax.dynamic_slice_in_dim(gsmall[8:12].reshape(-1), me * up_share, up_share, 0)

    own_states = jnp.where(sec == 0, states[0], states[1])
    other_states = swap(jnp.where(sec == 0, states[1], states[0]))
    both_states = jnp.concatenate(by_block(own_states, other_states), axis=0)
    grad_input = jnp.concatenate(by_block(dnext, swap(dnext)), axis=0)
    totals = (gqkv, gout, gup, gdown, columns[:6], columns[6:], gup_bias)
    return (both_states[None], grad_input) + tuple(member[None] for member in totals)


def solution(mesh):
    placed = (
        P("dp", None),
        P("dp", None),
        P("section", "dp", None),
        P("section", None, None),
        P("section", None, None),
        P("section", None, None),
        P("section", None, None),
        P("section", None, None),
        P("section", None, None),
        P("section", None),
    )
    return jax.shard_map(
        local,
        mesh=mesh,
        in_specs=placed,
        out_specs=(
            P("section", "dp", None),
            P("dp", None),
            P("section", "dp", None),
            P("section", "dp", None),
            P("section", "dp", None),
            P("section", "dp", None),
            P("section", None, "dp"),
            P("section", None, "dp"),
            P("section", "dp"),
        ),
        check_vma=False,
    )
```

time: 1400 us -> 335 us (0.24)
  waiting for transfers between devices: 713 us -> 8.85 us
  Pallas kernels: 0 us -> 289 us
  matrix products: 274 us -> 0 us
  other arithmetic: 155 us -> 15.6 us
  local copies, waits for them, and re-layouts: 152 us -> 16.7 us
  blocking collectives: 77.6 us -> 0 us
  between operations: 19 us -> 0.94 us
    reduce_scatter x4 -> x0, waiting for transfers between devices: 637 us -> none  [the longest x1 177 us: local(): lax.psum_scatter(grad_down, 'dp', scatter_dimension=0, tiled=True)]
    pallas_call x0 -> x5, Pallas kernels: none -> 289 us  [the longest x1 157 us: sum_products(): pl.pallas_call(sum_kernel, out_shape=(shaped((share, 3 * width)), shaped(...]
    dot_general x57 -> x0, matrix products: 274 us -> none  [the longest x12 59.1 us: times_transposed(): lax.dot_general(left_side, right_side, (((1,), (1,)), ((), ())), preferre...]
    unnamed x1 -> x0, blocking collectives: 77.6 us -> none
    unnamed x9 -> x0, waiting for transfers between devices: 76.6 us -> none
    reduce_sum x26 -> x0, other arithmetic: 40.1 us -> none  [the longest x3 10.6 us: attend_forward(): jnp.sum(jnp.exp(scores - maximum), axis=-1, keepdims=True)]
    convert_element_type x10 -> x0, other arithmetic: 36 us -> none  [the longest x3 21.5 us: attend_backward(): score_gradient = (attention_weight * (grad_weights - jnp.sum(attention_we...]
    another operation x18 -> x2, other arithmetic: 35.5 us -> 0.73 us  [local(): small = jnp.stack(dsmalls)]
  transfers between devices with their start and end apart: 11 -> 8, of which waited for: 5 -> 1; matrix products, arithmetic and copies ran while one was open for 13% -> 8% of each run, Pallas kernels for 0% -> 47%
where the time goes in v1:
time: 335 us; the launch traced here: 334 us
  Pallas kernels  289 us (86%)
  local copies, waits for them, and re-layouts  16.7 us (5%)
  other arithmetic  15.6 us (5%)
  waiting for transfers between devices  8.85 us (3%)
    pallas_call x1, Pallas kernels, sum_products(): pl.pallas_call(sum_kernel, out_shape=(shaped((share, 3 * width)), shaped(...  157 us
    pallas_call x2, Pallas kernels, block_backward(): pl.pallas_call(functools.partial(backward_kernel, block), out_shape=(shap...  69.1 us
    pallas_call x2, Pallas kernels, block_forward(): pl.pallas_call(functools.partial(forward_kernel, block), out_shape=(shape...  63.6 us
    ppermute x8, waiting for transfers between devices, swap(): return lax.ppermute(value, 'section', [(0, 1), (1, 0)])  8.85 us
    unnamed x48, local copies, waits for them, and re-layouts  7.9 us
  transfers between devices with their start and end apart: 8, of which 1 were waited for; matrix products, arithmetic and copies ran while one was open for 8% of the time, Pallas kernels for 47%

profile of v1, /device:TPU:0, one launch (start us, length us, event | category | flops | bytes accessed | tf_op | source)
XLA Modules:
  0.0 334.0 jit_solution(4469131744332510862)
XLA Ops:
  0.7 0.5 collective-permute-start.3
  1.3 0.4 collective-permute-start.1
  1.7 0.5 broadcast.22
  2.2 1.4 reduce.11
  3.6 0.7 copy.33
  4.3 1.3 pad_maximum_fusion.2
  5.7 0.4 collective-permute-start.2
  6.2 0.9 compare_reduce_fusion
  7.1 1.3 constant_dynamic-slice_fusion.1.segr_ref
  8.4 0.7 fusion.2
  9.1 0.9 constant_dynamic-slice_fusion.2.x_ref.dnext_ref.refs_0_
  10.0 0.7 add_convert_fusion
  10.7 0.9 copy.20.segc_ref
  11.6 1.5 copy.21.first_ref
  13.1 0.6 pad.16.clone
  13.8 8.8 %collective-permute-done = f32[12,768]{1,0:T(8,128)} collective-permute-done((f32[12,768]{1,0:T(8,128)}, f32[12,768]{1,0:T(8,128)}, u32[]{:S(2)}, u32[]{:S(2)}) %collective-permute-start) | collective-permute-done | bytes 36896 | tf_op jit(solution)/shard_map/ppermute | solution.py:582
  22.6 0.4 collective-permute-start.6
  23.0 0.8 broadcast_select_fusion.6
  23.9 0.6 copy.30
  24.5 0.6 copy.31
  25.1 1.3 pad_maximum_fusion.4
  26.4 1.5 bitcast_select_fusion
  28.0 1.0 copy-done.2
  29.0 31.9 %forward0.1 = (bf16[512,2304]{1,0:T(8,128)(2,1)}, bf16[512,768]{1,0:T(8,128)(2,1)}, f32[6,2,512]{2,1,0:T(2,128)}, f32[512,768]{1,0:T(8,128)}, f32[512,128]{1,0:T...) custom-call(bf16[512,768]{1,0:T(8,128)(2,1)} %constant_dynamic-slice, ...), custom_call_target="tpu_custom_call" | custom-call | tf_op jit(solution)/shard_map/forward0/pallas_call | solution.py:309
  60.8 31.7 %forward1.1 = (bf16[512,2304]{1,0:T(8,128)(2,1)}, bf16[512,768]{1,0:T(8,128)(2,1)}, f32[6,2,512]{2,1,0:T(2,128)}, f32[512,768]{1,0:T(8,128)}, f32[512,128]{1,0:T...) custom-call(bf16[512,768]{1,0:T(8,128)(2,1)} %get-tuple-element.52.x, ...), custom_call_target="tpu_custom_call" | custom-call | tf_op jit(solution)/shard_map/forward1/pallas_call | solution.py:309
  92.6 34.4 %backward1.1 = (f32[512,768]{1,0:T(8,128)}, bf16[512,2304]{1,0:T(8,128)(2,1)}, bf16[512,768]{1,0:T(8,128)(2,1)}, bf16[512,3072]{1,0:T(8,128)(2,1)}, bf16[512,768...) custom-call(bf16[512,768]{1,0:T(8,128)(2,1)} %get-tuple-element.113.cot_ref, ...), custom_call_target="tpu_custom_call" | custom-call | tf_op jit(solution)/shard_map/backward1/pallas_call | solution.py:332
  127.0 34.7 %backward0.1 = (f32[512,768]{1,0:T(8,128)}, bf16[512,2304]{1,0:T(8,128)(2,1)}, bf16[512,768]{1,0:T(8,128)(2,1)}, bf16[512,3072]{1,0:T(8,128)(2,1)}, bf16[512,768...) custom-call(bf16[512,768]{1,0:T(8,128)(2,1)} %get-tuple-element.114.cot_ref, ...), custom_call_target="tpu_custom_call" | custom-call | tf_op jit(solution)/shard_map/backward0/pallas_call | solution.py:332
  161.7 0.2 collective-permute-start.7
  161.9 1.0 broadcast_select_fusion.4
  162.9 0.4 collective-permute-start.5
  163.3 0.7 reduce.13
  164.0 0.7 reduce.12
  164.8 0.6 pad_maximum_fusion.1.refs_16_
  165.4 156.8 %sum_products.1 = (f32[48,2304]{1,0:T(8,128)}, f32[48,768]{1,0:T(8,128)}, f32[48,3072]{1,0:T(8,128)}, f32[192,768]{1,0:T(8,128)}, f32[16,768]{1,0:T(8,128)}) custom-call(bf16[512,768]{1,0:T(8,128)(2,1)} %constant_dynamic-slice_fusion.2.x_ref.dnext_ref.refs_0_, bf16[512,2304]{1,0:T(8,128)(2,1)} %get-tuple-element.72.refs_1_, ...), custom_call_target="tpu_custom_call" | custom-call | tf_op jit(solution)/shard_map/sum_products/pallas_call | solution.py:541
  322.2 0.7 slice.54
  323.0 0.7 slice.57
  323.8 0.6 copy.28
  324.4 0.6 dynamic_slice.30
  325.0 0.6 slice_bitcast_fusion.3
  325.6 1.3 broadcast_select_fusion.3
  326.9 1.2 maximum_bitcast_fusion
  328.1 0.7 copy-done.7
  328.8 0.2 broadcast_select_fusion.1
  329.1 1.9 pad_maximum_fusion
  330.9 0.8 copy.38
  331.7 0.7 copy.39
  332.4 0.8 copy.40
  333.2 0.8 copy.41
  (60 shorter events, 0.6 us)
Async XLA Ops:
  0.6 8.4 %copy-start = (bf16[1024,768]{1,0:T(8,128)(2,1)S(1)}, bf16[1024,768]{1,0:T(8,128)(2,1)}, u32[]{:S(2)}) copy-start(bf16[1024,768]{1,0:T(8,128)(2,1)} %param.10) | copy-start | bytes 4718596
  0.7 27.3 %collective-permute-start.3 = (bf16[768,3072]{1,0:T(8,128)(2,1)}, bf16[768,3072]{1,0:T(8,128)(2,1)}, u32[]{:S(2)}, u32[]{:S(2)}) collective-permute-start(bf16[768,3072]{1,0:T(8,128)(2,1)} %bitcast.39), channel_id=1, source_target_pairs={{0,16},{16,0},{1,17},{17,1},{2,18},{18,2},{3,19},{19,3},{4,20},{20... | collective-permute-start | bytes 14155784 | tf_op jit(solution)/shard_map/ppermute | solution.py:582
  1.2 26.8 %collective-permute-start.4 = (bf16[3072,768]{1,0:T(8,128)(2,1)}, bf16[3072,768]{1,0:T(8,128)(2,1)}, u32[]{:S(2)}, u32[]{:S(2)}) collective-permute-start(bf16[3072,768]{1,0:T(8,128)(2,1)} %bitcast.44), channel_id=1, source_target_pairs={{0,16},{16,0},{1,17},{17,1},{2,18},{18,2},{3,19},{19,3},{4,20},{20... | collective-permute-start | bytes 14155784 | tf_op jit(solution)/shard_map/ppermute | solution.py:582
  1.3 26.7 %collective-permute-start.1 = (bf16[768,2304]{1,0:T(8,128)(2,1)}, bf16[768,2304]{1,0:T(8,128)(2,1)}, u32[]{:S(2)}, u32[]{:S(2)}) collective-permute-start(bf16[768,2304]{1,0:T(8,128)(2,1)} %bitcast.49), channel_id=1, source_target_pairs={{0,16},{16,0},{1,17},{17,1},{2,18},{18,2},{3,19},{19,3},{4,20},{20... | collective-permute-start | bytes 10616840 | tf_op jit(solution)/shard_map/ppermute | solution.py:582
  4.3 1.4 copy-start.13
  5.7 17.0 %collective-permute-start = (f32[12,768]{1,0:T(8,128)}, f32[12,768]{1,0:T(8,128)}, u32[]{:S(2)}, u32[]{:S(2)}) collective-permute-start(f32[12,768]{1,0:T(8,128)} %pad_maximum_fusion.2), channel_id=1, source_target_pairs={{0,16},{16,0},{1,17},{17,1},{2,18},{18,2},{3,19},{19,3},{4,20},{20... | collective-permute-start | bytes 110600 | tf_op jit(solution)/shard_map/ppermute | solution.py:582
  5.7 22.2 %collective-permute-start.2 = (bf16[768,768]{1,0:T(8,128)(2,1)}, bf16[768,768]{1,0:T(8,128)(2,1)S(1)}, u32[]{:S(2)}, u32[]{:S(2)}) collective-permute-start(bf16[768,768]{1,0:T(8,128)(2,1)} %bitcast.54), channel_id=1, source_target_pairs={{0,16},{16,0},{1,17},{17,1},{2,18},{18,2},{3,19},{19,3},{4,20},{20... | collective-permute-start | bytes 3538952 | tf_op jit(solution)/shard_map/ppermute | solution.py:582
  6.2 3.8 %copy-start.5 = (bf16[1,1024,768]{2,1,0:T(8,128)(2,1)S(1)}, bf16[1,1024,768]{2,1,0:T(8,128)(2,1)}, u32[]{:S(2)}) copy-start(bf16[1,1024,768]{2,1,0:T(8,128)(2,1)} %param.12) | copy-start | bytes 4718596
  10.0 16.4 %copy-start.6 = (bf16[1,1024,768]{2,1,0:T(8,128)(2,1)S(1)}, bf16[1,1024,768]{2,1,0:T(8,128)(2,1)}, u32[]{:S(2)}) copy-start(bf16[1,1024,768]{2,1,0:T(8,128)(2,1)} %param.12) | copy-start | bytes 4718596
  22.6 3.8 %collective-permute-start.6 = (bf16[512,768]{1,0:T(8,128)(2,1)S(1)}, bf16[512,768]{1,0:T(8,128)(2,1)S(1)}, u32[]{:S(2)}, u32[]{:S(2)}) collective-permute-start(bf16[512,768]{1,0:T(8,128)(2,1)S(1)} %dynamic-slice_bitcast_fusion), channel_id=1, source_target_pairs={{0,16},{16,0},{1,17},{17,1},{2,18},{18,2},{3,19},{19,3},{4,20},{20... | collective-permute-start | bytes 2359304 | tf_op jit(solution)/shard_map/ppermute | solution.py:582
  23.8 4.1 %copy-start.10 = (f32[12,768]{1,0:T(8,128)}, f32[12,768]{1,0:T(8,128)S(1)}, u32[]{:S(2)}) copy-start(f32[12,768]{1,0:T(8,128)S(1)} %get-tuple-element.118.small_ref) | copy-start | bytes 110596
  23.8 4.1 %copy-start.11 = (f32[12,768]{1,0:T(8,128)}, f32[12,768]{1,0:T(8,128)S(1)}, u32[]{:S(2)}) copy-start(f32[12,768]{1,0:T(8,128)S(1)} %get-tuple-element.117.small_ref) | copy-start | bytes 110596
  27.9 1.0 copy-start.2
  127.0 35.0 %copy-start.3 = (bf16[512,768]{1,0:T(8,128)(2,1)S(1)}, bf16[512,768]{1,0:T(8,128)(2,1)}, u32[]{:S(2)}) copy-start(bf16[512,768]{1,0:T(8,128)(2,1)} %get-tuple-element.51) | copy-start | bytes 2359300
  127.0 35.0 %copy-start.4 = (bf16[512,768]{1,0:T(8,128)(2,1)S(1)}, bf16[512,768]{1,0:T(8,128)(2,1)}, u32[]{:S(2)}) copy-start(bf16[512,768]{1,0:T(8,128)(2,1)} %get-tuple-element.53) | copy-start | bytes 2359300
  161.7 1.6 copy-start.18
  161.7 2.3 copy-start.16
  161.7 2.3 copy-start.17
  161.7 3.0 copy-start.15
  161.7 166.4 %collective-permute-start.7 = (f32[512,768]{1,0:T(8,128)}, f32[512,768]{1,0:T(8,128)S(1)}, u32[]{:S(2)}, u32[]{:S(2)}) collective-permute-start(f32[512,768]{1,0:T(8,128)} %get-tuple-element.71), channel_id=1, source_target_pairs={{0,16},{16,0},{1,17},{17,1},{2,18},{18,2},{3,19},{19,3},{4,20},{20... | collective-permute-start | bytes 4718600 | tf_op jit(solution)/shard_map/ppermute | solution.py:582
  162.9 162.7 %collective-permute-start.5 = (bf16[512,768]{1,0:T(8,128)(2,1)}, bf16[512,768]{1,0:T(8,128)(2,1)}, u32[]{:S(2)}, u32[]{:S(2)}) collective-permute-start(bf16[512,768]{1,0:T(8,128)(2,1)} %broadcast_select_fusion.4), channel_id=1, source_target_pairs={{0,16},{16,0},{1,17},{17,1},{2,18},{18,2},{3,19},{19,3},{4,20},{20... | collective-permute-start | bytes 2359304 | tf_op jit(solution)/shard_map/ppermute | solution.py:582
  326.9 2.0 copy-start.7
  329.0 1.9 copy-start.12
  329.1 2.7 copy-start.14
  330.9 1.4 copy-start.9
  330.9 2.3 copy-start.8
  330.9 3.1 copy-start.1
